TPU v7x, 768 devices: a whole 4x8x12 slice. The times are simulated.
768 devices in a mesh: blk: 24 (over y, z_hi), row: 32 (over x, z_lo, core).
Axes of the slice: x: 4, y: 8, z: 12 (z_hi: 3, z_lo: 4; z = z_hi * 4 + z_lo), core: 2. Of those that a mesh axis runs over, the one named last changes fastest.
Arguments:
- features: float32 [64, 98304], P(None, ('blk', 'row')), may hold values from -6 to 6
- reorder: int32 [768, 128], P(('blk', 'row')), may hold values from 0 to 127, each once within a row
- tile_rows: int32 [24, 32, 64], P('blk', 'row'), may hold values from 0 to 31
- tile_cols: int32 [24, 32, 64], P('blk', 'row'), may hold values from 0 to 23
- tile_vals: float32 [24, 32, 64, 128, 128], P('blk', 'row')
- tile_count: int32 [24, 32], P('blk', 'row'), may hold values from 1 to 64, as said below
Outputs:
- hop_one: float32 [64, 98304], P(None, ('blk', 'row'))
- hop_two: float32 [64, 98304], P(None, ('blk', 'row'))
Inputs may be any that keep to these rules, and one draw needn't show every extreme that they name: `tile_count`: some device has all 64 slots live.
All inputs are finite; a program needn't handle non-finite values.
Results may differ from a plain program's by a relative error of at most 0.0003.
Values sent between devices are 32-bit elements; how exact they have to be, the bound alone decides.
A program may use at most 32 MiB of HBM per device.

v0:
```python
import jax
import jax.numpy as jnp
from jax import lax
from jax.sharding import PartitionSpec as P


def propagate(local, rows, cols, vals, count):
    feat_count = local.shape[0]
    tile_size = vals.shape[-1]
    slots = vals.shape[0]
    row_tiles = lax.axis_size("row") * local.shape[1] // tile_size
    gathered = lax.all_gather(local, "blk", axis=1, tiled=True)
    panel = gathered.reshape(feat_count, -1, tile_size)
    picked = jnp.take(panel, cols, axis=1)
    contrib = jnp.einsum("ftj,tij->fti", picked, vals, precision=lax.Precision.HIGHEST)
    live = (jnp.arange(slots) < count).astype(jnp.float32)
    contrib = contrib * live[None, :, None]
    onehot = (rows[:, None] == jnp.arange(row_tiles)[None, :]).astype(jnp.float32)
    placed = jnp.einsum("fti,tr->fri", contrib, onehot, precision=lax.Precision.HIGHEST)
    partial_rows = placed.reshape(feat_count, row_tiles * tile_size)
    totals = lax.psum(partial_rows, "row")
    width = local.shape[1]
    return lax.dynamic_slice_in_dim(totals, lax.axis_index("row") * width, width, 1)


def shards(features, reorder, tile_rows, tile_cols, tile_vals, tile_count):
    order = reorder[0]
    rows = tile_rows[0, 0]
    cols = tile_cols[0, 0]
    vals = tile_vals[0, 0]
    count = tile_count[0, 0]
    reordered = jnp.take(features, order, axis=1)
    first = propagate(reordered, rows, cols, vals, count)
    second = propagate(first, rows, cols, vals, count)
    empty = jnp.zeros(features.shape, jnp.float32)
    hop_one = empty.at[:, order].set(first)
    hop_two = empty.at[:, order].set(second)
    return (hop_one, hop_two)


def solution(mesh):
    return jax.shard_map(
        shards,
        mesh=mesh,
        in_specs=(
            P(None, ("blk", "row")),
            P(("blk", "row"), None),
            P("blk", "row", None),
            P("blk", "row", None),
            P("blk", "row", None, None, None),
            P("blk", "row"),
        ),
        out_specs=(P(None, ("blk", "row")), P(None, ("blk", "row"))),
        check_vma=False,
    )
```

profile of v0, /device:TPU:1, one launch (start us, length us, event | category | flops | bytes accessed | tf_op | source)
XLA Modules:
  0.0 888.1 jit_solution(7631207696692841163)
XLA Ops:
  7.2 0.7 fusion.36
  7.9 0.7 compare_and_fusion.1
  8.5 0.7 compare_and_fusion
  9.2 0.7 compare_select_fusion
  10.5 0.8 copy.8
  11.4 0.6 gather_fusion
  12.0 0.1 select_bitcast_fusion
  12.1 112.2 %all_gather.6 = f32[64,3072]{0,1:T(8,128)S(1)} all-gather(f32[64,128]{0,1:T(8,128)S(1)} %select_bitcast_fusion), channel_id=1, replica_groups=mesh['blk'=24,'row'=32] {'blk'}, dimensions={1}, use_global_device_ids=true | all-gather | bytes 819200 | tf_op jit(solution)/shard_map/all_gather | solution.py:12
  124.4 2.7 gather_fusion.1
  127.1 10.6 %fusion.3 = f32[64,64,128]{2,1,0:T(8,128)S(1)} fusion(f32[1,1,64,128,128]{4,3,2,1,0:T(8,128)} %param.12, f32[64,64,128]{1,2,0:T(8,128)} %gather_fusion.1, pred[64]{0:T(512)(128)(4,1)S(1)} %compare_and_fusion), kind=kOutput, calls=%fused_computation.8 | convolution fusion | flops 805830656 | bytes 8388672 | tf_op jit(solution)/shard_map/ftj,tij->fti/dot_general | solution.py:15
  137.7 2.0 fusion.16
  139.7 2.1 copy.15
  141.9 318.5 %all-reduce.3.cloned.1.call-done = f32[64,4096]{0,1:T(8,128)} async-done(((f32[64,4096]{0,1:T(8,128)}), f32[64,4096]{0,1:T(8,128)}) %all-reduce.3.cloned.1.call-update) | async-done | bytes 1048592 | tf_op jit(solution)/shard_map/psum | solution.py:21
  460.4 0.8 constant_dynamic-slice_fusion
  461.3 94.7 %all_gather.7 = f32[64,3072]{0,1:T(8,128)S(1)} all-gather(f32[64,128]{0,1:T(8,128)S(1)} %constant_dynamic-slice_fusion), channel_id=1, replica_groups=mesh['blk'=24,'row'=32] {'blk'}, dimensions={1}, use_global_device_ids=true | all-gather | bytes 819200 | tf_op jit(solution)/shard_map/all_gather | solution.py:12
  556.0 2.7 gather_fusion.2
  558.7 10.5 %fusion = f32[64,64,128]{2,1,0:T(8,128)S(1)} fusion(f32[1,1,64,128,128]{4,3,2,1,0:T(8,128)} %param.12, f32[64,64,128]{1,2,0:T(8,128)} %gather_fusion.2, pred[64]{0:T(512)(128)(4,1)S(1)} %compare_and_fusion), kind=kOutput, calls=%fused_computation.5 | convolution fusion | flops 805830656 | bytes 8388672 | tf_op jit(solution)/shard_map/ftj,tij->fti/dot_general | solution.py:15
  569.3 2.0 fusion.19
  571.3 2.0 copy.16
  573.3 1.2 scatter_custom_fusion
  574.6 0.7 copy.11
  575.3 304.1 %all-reduce.5.cloned.1.call-done = f32[64,4096]{0,1:T(8,128)} async-done(((f32[64,4096]{0,1:T(8,128)}), f32[64,4096]{0,1:T(8,128)}) %all-reduce.5.cloned.1.call-update) | async-done | bytes 1048592 | tf_op jit(solution)/shard_map/psum | solution.py:21
  879.3 1.2 scatter_custom_fusion.1
  880.5 0.7 copy.12
  (9 shorter events, 0.1 us)
Async XLA Ops:
  7.2 453.3 %all-reduce.3.cloned.1.call-start = ((), (), s32[]{:S(2)}) async-start(), calls=%async_computation | async-start | bytes 4194304 | tf_op jit(solution)/shard_map/psum | solution.py:21
  127.1 10.6 %copy-start = (s32[1,1,64]{2,1,0:T(1,128)S(1)}, s32[1,1,64]{2,1,0:T(1,128)}, u32[]{:S(2)}) copy-start(s32[1,1,64]{2,1,0:T(1,128)} %param.10) | copy-start | bytes 772
  141.8 737.5 %all-reduce.5.cloned.1.call-start = ((), (), s32[]{:S(2)}) async-start(), calls=%async_computation.1 | async-start | bytes 4194304 | tf_op jit(solution)/shard_map/psum | solution.py:21
Sparse Core Ops, SparseCore 0:
  141.9 318.4 all-reduce.2
  573.5 305.8 all-reduce.4
where the time goes:
time: 888 us
  waiting for transfers between devices  623 us (70%)
  blocking collectives  207 us (23%)
  matrix products  25.2 us (3%)
  local copies, waits for them, and re-layouts  15.7 us (2%)
  between operations  14.8 us (2%)
    psum x2, waiting for transfers between devices, propagate(): totals = lax.psum(partial_rows, 'row')  623 us
    all_gather x2, blocking collectives, propagate(): gathered = lax.all_gather(local, 'blk', axis=1, tiled=True)  207 us
    dot_general x2, matrix products, propagate(): jnp.einsum('ftj,tij->fti', picked, vals, precision=lax.Precision.HIGHEST)  21.1 us
  transfers between devices with their start and end apart: 2, of which 2 were waited for; matrix products, arithmetic and copies ran while one was open for 0% of the time, Pallas kernels for 0%

commit v1 on v0

v1 whole, which is shorter than its diff:
```python
import jax
import jax.numpy as jnp
from jax import lax
from jax.experimental import pallas as pl
from jax.experimental.pallas import tpu as pltpu
from jax.sharding import PartitionSpec as P

MESH = pl.DeviceIdType.MESH
F32 = jnp.float32
BF16 = jnp.bfloat16
NY, NZH, NX, NZL = 8, 3, 4, 4
SLOTS = 64
FEAT = 64
TILE = 128
FAR = (4,)
NEAR = tuple(d for d in range(1, NY) if d not in FAR)


def device(y, zh, x, zl, core):
    return (y * NZH + zh, (x * NZL + zl) * 2 + core)


def kernel(feat_hbm, reorder_hbm, rows_hbm, cols_hbm, count_hbm, vals_hbm,
           hop1_ref, hop2_ref,
           feat, reorder, rows, cols, count, vals, table, plan, weights,
           panel, split, seg, send_a, got_a, own_a, send_b, got_b, keep_b, send_c, got_c,
           in_sem, val_sem, plan_sem,
           s_z, r_z, s_y, r_y, r_far, s_ry, r_ry, s_rz, r_rz,
           s_a, r_a, s_b, r_b, s_c, r_c):
    blk = lax.axis_index("blk")
    row = lax.axis_index("row")
    y, zh = blk // NZH, lax.rem(blk, NZH)
    x, zl, core = row // (2 * NZL), lax.rem(row // 2, NZL), lax.rem(row, 2)

    def y_peer(d):
        return device(lax.rem(y + d, NY), zh, x, zl, core)

    def zh_peer(d):
        return device(y, lax.rem(zh + d, NZH), x, zl, core)

    def x_peer(d):
        return device(y, zh, lax.rem(x + d, NX), zl, core)

    def zl_peer(d):
        return device(y, zh, x, lax.rem(zl + d, NZL), core)

    sibling = device(y, zh, x, zl, 1 - core)
    peers = ([y_peer(d) for d in range(1, NY)] + [zh_peer(d) for d in range(1, NZH)] + [x_peer(d) for d in range(1, NX)]
             + [zl_peer(d) for d in range(1, NZL)] + [sibling])
    barrier = pltpu.get_barrier_semaphore()
    for peer in peers:
        pl.semaphore_signal(barrier, inc=1, device_id=peer, device_id_type=MESH)

    loads = [
        pltpu.make_async_copy(feat_hbm, feat, in_sem.at[0]),
        pltpu.make_async_copy(reorder_hbm, reorder, in_sem.at[1]),
        pltpu.make_async_copy(rows_hbm, rows, in_sem.at[2]),
        pltpu.make_async_copy(cols_hbm, cols, in_sem.at[3]),
        pltpu.make_async_copy(count_hbm, count, in_sem.at[4]),
    ]
    for load in loads:
        load.start()
    halves = [pltpu.make_async_copy(vals_hbm.at[0, 0, pl.ds(h * 32, 32)], vals.at[pl.ds(h * 32, 32)], val_sem.at[h])
              for h in range(2)]
    for load in halves:
        load.start()
    for load in loads:
        load.wait()

    onehot = (lax.broadcasted_iota(jnp.int32, (TILE, TILE), 0) == reorder[...]).astype(F32)
    panel[0, blk] = lax.dot_general(feat[...], onehot, (((1,), (0,)), ((), ())), precision=lax.Precision.HIGHEST,
                                    preferred_element_type=F32)
    pl.semaphore_wait(barrier, len(peers))

    def remote(src, dst, send, recv, peer):
        return pltpu.make_async_remote_copy(src_ref=src, dst_ref=dst, send_sem=send, recv_sem=recv, device_id=peer,
                                            device_id_type=MESH)

    def await_bytes(ref, sem):
        pltpu.make_async_copy(ref, ref, sem).wait()

    def gather_own(h):
        mine = panel.at[h, blk]
        for d in range(1, NZH):
            remote(mine, mine, s_z.at[h], r_z.at[h], zh_peer(d)).start()
        for d in (4, 3, 5, 2, 6, 1, 7):
            recv = r_far.at[h, FAR.index(d)] if d in FAR else r_y.at[h]
            remote(mine, mine, s_y.at[h], recv, y_peer(d)).start()

    def gather_relay_y(h):
        await_bytes(panel.at[h, pl.ds(0, NZH - 1)], r_z.at[h])
        for d in sorted(NEAR, key=lambda d: -min(d, NY - d)):
            for e in range(1, NZH):
                block = panel.at[h, y * NZH + lax.rem(zh + e, NZH)]
                remote(block, block, s_ry.at[h], r_ry.at[h], y_peer(d)).start()

    def gather_relay_z(h):
        for n, d in enumerate(FAR):
            await_bytes(panel.at[h, 0], r_far.at[h, n])
            block = panel.at[h, lax.rem(y + NY - d, NY) * NZH + zh]
            for e in range(1, NZH):
                remote(block, block, s_rz.at[h], r_rz.at[h], zh_peer(e)).start()

    def gather_end(h):
        await_bytes(panel.at[h, pl.ds(0, len(NEAR))], r_y.at[h])
        await_bytes(panel.at[h, pl.ds(0, 2 * len(FAR))], r_rz.at[h])
        await_bytes(panel.at[h, pl.ds(0, 2 * len(NEAR))], r_ry.at[h])

    def split_panel(h):
        def one(c, carry):
            block = panel[h, c]
            high = block.astype(BF16)
            split[c, :, 0:TILE] = high
            split[c, :, TILE:2 * TILE] = (block - high.astype(F32)).astype(BF16)
            return carry
        lax.fori_loop(0, NY * NZH, one, 0, unroll=4)

    def prepare(first):
        def one(t, carry):
            tile = vals[t].T
            high = tile.astype(BF16)
            weights[t, :, 0:TILE] = high
            weights[t, :, TILE:2 * TILE] = (tile - high.astype(F32)).astype(BF16)
            return carry
        lax.fori_loop(first, first + 32, one, 0, unroll=4)

    def plan_slots():
        lane = lax.broadcasted_iota(jnp.int32, (1, TILE), 1)
        padded = jnp.concatenate([rows[0], jnp.zeros((1, TILE - SLOTS), jnp.int32)], axis=1)
        group = jnp.where(lane < count[0, 0], padded, 32)
        key = group * SLOTS + lane + jnp.where(lane < SLOTS, 0, 4096)
        across = jnp.broadcast_to(key, (TILE, TILE))
        down = across.T
        rank = jnp.sum(jnp.where(across < down, 1, 0), axis=1, keepdims=True)
        lanes = lax.broadcasted_iota(jnp.int32, (TILE, TILE), 1)
        order = jnp.sum(jnp.where(rank == lanes, down, 0), axis=0, keepdims=True)
        upto = jnp.sum(jnp.where(down < (lanes + 1) * SLOTS, 1, 0), axis=0, keepdims=True)
        before = jnp.sum(jnp.where(down < lanes * SLOTS, 1, 0), axis=0, keepdims=True)
        table[0:1, :] = order
        table[1:2, :] = jnp.maximum(upto - 1, 0)
        table[2:3, :] = upto - before
        copy = pltpu.make_async_copy(table, plan, plan_sem)
        copy.start()
        return copy

    def multiply():
        def one(k, carry):
            total, last = carry
            key = plan[0, k]
            slot = key & (SLOTS - 1)
            group = key >> 6
            column = jnp.clip(cols[0, 0, slot], 0, NY * NZH - 1)
            left = split[column]
            tile = weights[slot]
            both = lax.dot_general(left, jnp.concatenate([tile, tile], axis=0), (((1,), (0,)), ((), ())),
                                   preferred_element_type=F32)
            term = both[:, 0:TILE] + both[:, TILE:2 * TILE]
            total = jnp.where(group == last, total, 0.0) + term
            seg[k] = total
            return total, group
        lax.fori_loop(0, SLOTS, one, (jnp.zeros((FEAT, TILE), F32), jnp.int32(-1)), unroll=8)

    def row_total(r):
        return jnp.where(plan[2, r] > 0, seg[plan[1, r] & (SLOTS - 1)], 0.0)

    def scatter_sum(h):
        for n in range(NZL):
            zt = lax.rem(zl + n + 1, NZL)
            for xt in range(NX):
                r = (xt * NZL + zt) * 2
                send_a[h, n, xt] = row_total(r + 1 - core)
                own_a[n, xt] = row_total(r + core)
            remote(send_a.at[h, n], got_a.at[h, n], s_a.at[h], r_a.at[h, n], sibling).start()
        for n in range(NZL):
            await_bytes(got_a.at[h, n], r_a.at[h, n])
            for d in (2, 1, 3):
                xt = lax.rem(x + d, NX)
                send_b[h, n, d - 1] = own_a[n, xt] + got_a[h, n, xt]
                remote(send_b.at[h, n, d - 1], got_b.at[h, n, d - 1], s_b.at[h], r_b.at[h, n], x_peer(d)).start()
            keep_b[n] = own_a[n, x] + got_a[h, n, x]
        for n in range(NZL):
            await_bytes(got_b.at[h, n], r_b.at[h, n])
            part = (keep_b[n] + got_b[h, n, 0]) + (got_b[h, n, 1] + got_b[h, n, 2])
            if n < NZL - 1:
                send_c[h, n] = part
                remote(send_c.at[h, n], got_c.at[h, n], s_c.at[h], r_c.at[h], zl_peer(n + 1)).start()
        await_bytes(got_c.at[h], r_c.at[h])
        return part + (got_c[h, 0] + got_c[h, 1] + got_c[h, 2])

    def sends_end(h):
        await_bytes(panel.at[h, pl.ds(0, NZH - 1)], s_z.at[h])
        await_bytes(panel.at[h, pl.ds(0, NY - 1)], s_y.at[h])
        await_bytes(panel.at[h, pl.ds(0, 2 * len(NEAR))], s_ry.at[h])
        await_bytes(panel.at[h, pl.ds(0, 2 * len(FAR))], s_rz.at[h])
        await_bytes(send_a.at[h], s_a.at[h])
        await_bytes(send_b.at[h], s_b.at[h])
        await_bytes(send_c.at[h], s_c.at[h])

    def restored(field):
        return lax.dot_general(field, onehot, (((1,), (1,)), ((), ())), precision=lax.Precision.HIGHEST,
                               preferred_element_type=F32)

    gather_own(0)
    copy = plan_slots()
    halves[0].wait()
    prepare(0)
    gather_relay_y(0)
    gather_relay_z(0)
    halves[1].wait()
    prepare(32)
    copy.wait()
    gather_end(0)
    split_panel(0)
    multiply()
    first = scatter_sum(0)
    panel[1, blk] = first
    gather_own(1)
    hop1_ref[...] = restored(first)
    gather_relay_y(1)
    gather_relay_z(1)
    gather_end(1)
    split_panel(1)
    multiply()
    second = scatter_sum(1)
    hop2_ref[...] = restored(second)
    sends_end(0)
    sends_end(1)


def shards(features, reorder, tile_rows, tile_cols, tile_vals, tile_count):
    dma = pltpu.SemaphoreType.DMA
    block = (FEAT, TILE)
    return pl.pallas_call(
        kernel,
        name="two_hops",
        out_shape=(jax.ShapeDtypeStruct(block, F32), jax.ShapeDtypeStruct(block, F32)),
        in_specs=[pl.BlockSpec(memory_space=pltpu.HBM)] * 6,
        out_specs=(pl.BlockSpec(memory_space=pltpu.VMEM), pl.BlockSpec(memory_space=pltpu.VMEM)),
        scratch_shapes=[
            pltpu.VMEM(block, F32),
            pltpu.VMEM((1, TILE), jnp.int32),
            pltpu.VMEM((1, 1, SLOTS), jnp.int32),
            pltpu.SMEM((1, 1, SLOTS), jnp.int32),
            pltpu.SMEM((1, 1), jnp.int32),
            pltpu.VMEM((SLOTS, TILE, TILE), F32),
            pltpu.VMEM((8, TILE), jnp.int32),
            pltpu.SMEM((8, TILE), jnp.int32),
            pltpu.VMEM((SLOTS, TILE, 2 * TILE), BF16),
            pltpu.VMEM((2, NY * NZH) + block, F32),
            pltpu.VMEM((NY * NZH, FEAT, 2 * TILE), BF16),
            pltpu.VMEM((SLOTS,) + block, F32),
            pltpu.VMEM((2, NZL, NX) + block, F32),
            pltpu.VMEM((2, NZL, NX) + block, F32),
            pltpu.VMEM((NZL, NX) + block, F32),
            pltpu.VMEM((2, NZL, NX - 1) + block, F32),
            pltpu.VMEM((2, NZL, NX - 1) + block, F32),
            pltpu.VMEM((NZL,) + block, F32),
            pltpu.VMEM((2, NZL - 1) + block, F32),
            pltpu.VMEM((2, NZL - 1) + block, F32),
            dma((5,)), dma((2,)), dma,
            dma((2,)), dma((2,)), dma((2,)), dma((2,)), dma((2, len(FAR))), dma((2,)), dma((2,)), dma((2,)), dma((2,)),
            dma((2,)), dma((2, NZL)), dma((2,)), dma((2, NZL)), dma((2,)), dma((2,)),
        ],
        compiler_params=pltpu.CompilerParams(collective_id=0, has_side_effects=True, vmem_limit_bytes=56 << 20),
        cost_estimate=pl.CostEstimate(flops=2 * 2 * 64 * 64 * 128 * 128 * 4, bytes_accessed=4 << 20, transcendentals=0),
    )(features, reorder, tile_rows, tile_cols, tile_count, tile_vals)


def solution(mesh):
    return jax.shard_map(
        shards,
        mesh=mesh,
        in_specs=(
            P(None, ("blk", "row")),
            P(("blk", "row"), None),
            P("blk", "row", None),
            P("blk", "row", None),
            P("blk", "row", None, None, None),
            P("blk", "row"),
        ),
        out_specs=(P(None, ("blk", "row")), P(None, ("blk", "row"))),
        check_vma=False,
    )
```

time: 888 us -> 83.8 us (0.09)
  waiting for transfers between devices: 623 us -> 0 us
  blocking collectives: 207 us -> 0 us
  Pallas kernels: 0 us -> 79.4 us
  matrix products: 25.2 us -> 0 us
  between operations: 14.8 us -> 1.29 us
  local copies, waits for them, and re-layouts: 15.7 us -> 2.75 us
    psum x2 -> x0, waiting for transfers between devices: 623 us -> none  [propagate(): totals = lax.psum(partial_rows, 'row')]
    all_gather x2 -> x0, blocking collectives: 207 us -> none  [propagate(): gathered = lax.all_gather(local, 'blk', axis=1, tiled=True)]
    pallas_call x0 -> x1, Pallas kernels: none -> 79.4 us  [shards(): pl.pallas_call(kernel, name='two_hops', out_shape=(jax.ShapeDtypeStruct(b...]
    dot_general x4 -> x0, matrix products: 25.2 us -> none  [the longest x2 21.1 us: propagate(): jnp.einsum('ftj,tij->fti', picked, vals, precision=lax.Precision.HIGHEST)]
  transfers between devices with their start and end apart: 2 -> 0, of which waited for: 2 -> 0; matrix products, arithmetic and copies ran while one was open for 0% -> 0% of each run, Pallas kernels for 0% -> 0%
where the time goes in v1:
time: 83.8 us; the launch traced here: 83.5 us
  Pallas kernels  79.4 us (95%)
  local copies, waits for them, and re-layouts  2.75 us (3%)
  between operations  1.29 us (2%)
    pallas_call x1, Pallas kernels, shards(): pl.pallas_call(kernel, name='two_hops', out_shape=(jax.ShapeDtypeStruct(b...  79.4 us
    unnamed x2, local copies, waits for them, and re-layouts  2.75 us

profile of v1, /device:TPU:1, one launch (start us, length us, event | category | flops | bytes accessed | tf_op | source)
XLA Modules:
  0.0 83.5 jit_solution(17083490406538824962)
XLA Ops:
  1.3 79.4 %two_hops.1 = (f32[64,128]{1,0:T(8,128)}, f32[64,128]{1,0:T(8,128)}) custom-call(f32[64,128]{1,0:T(8,128)} %feat_hbm.1, s32[1,128]{1,0:T(1,128)} %reorder_hbm.1, s32[1,1,64]{2,1,0:T(1,128)} %rows_hbm.1, s32[1,1,64]{2,1,0:T(1,128)} %cols_hbm.1, s32[1,1]{1,0:T(1,128)S(6)} %copy.10.count_hbm, f32[1,1,64,128,128]{4,3,2,1,0:T(8,128)} %vals_hbm.1), custom_call_target="tpu_custom_call" | custom-call | flops 1073741824 | bytes 4194304 | tf_op jit(solution)/shard_map/two_hops/pallas_call | solution.py:233
  80.7 1.4 %copy.11 = f32[64,128]{1,0:T(8,128)} copy(f32[64,128]{1,0:T(8,128)} %get-tuple-element.4) | data formatting | bytes 65536
  82.1 1.4 %copy.12 = f32[64,128]{1,0:T(8,128)} copy(f32[64,128]{1,0:T(8,128)} %get-tuple-element.5) | data formatting | bytes 65536

commit v2 on v1

v2 whole, which is shorter than its diff:
```python
import jax
import jax.numpy as jnp
from jax import lax
from jax.experimental import pallas as pl
from jax.experimental.pallas import tpu as pltpu
from jax.sharding import PartitionSpec as P

MESH = pl.DeviceIdType.MESH
F32 = jnp.float32
BF16 = jnp.bfloat16
NY, NZH, NX, NZL = 8, 3, 4, 4
SLOTS = 64
FEAT = 64
TILE = 128
FAR = (4, 3, 5)
NEAR = (2, 6, 1, 7)


def device(y, zh, x, zl, core):
    return (y * NZH + zh, (x * NZL + zl) * 2 + core)


def kernel(feat_hbm, reorder_hbm, rows_hbm, cols_hbm, count_hbm, vals_hbm,
           out_ref,
           feat, reorder, rows, cols, count, vals, table, plan, weights,
           panel, split, seg, send_a, got_a, send_b, got_b, keep_b, send_c, got_c,
           in_sem, val_sem, plan_sem,
           s_g, r_z, r_far, r_near, r_relay, s_a, r_a, s_b, r_b, s_c, r_c):
    blk = lax.axis_index("blk")
    row = lax.axis_index("row")
    y, zh = blk // NZH, lax.rem(blk, NZH)
    x, zl, core = row >> 3, (row >> 1) & (NZL - 1), row & 1
    order = (jnp.where(zl < 2, 3, 0), jnp.where(zl < 2, 2, 1),
             jnp.where(zl == 0, 1, jnp.where(zl == 1, 0, jnp.where(zl == 2, 3, 2))), zl)

    def y_peer(d):
        return device((y + d) & (NY - 1), zh, x, zl, core)

    def zh_peer(d):
        return device(y, jnp.where(zh + d >= NZH, zh + d - NZH, zh + d), x, zl, core)

    def x_peer(d):
        return device(y, zh, (x + d) & (NX - 1), zl, core)

    def zl_peer(t):
        return device(y, zh, x, t, core)

    sibling = device(y, zh, x, zl, 1 - core)
    loads = [
        pltpu.make_async_copy(feat_hbm, feat, in_sem.at[0]),
        pltpu.make_async_copy(reorder_hbm, reorder, in_sem.at[1]),
        pltpu.make_async_copy(rows_hbm, rows, in_sem.at[2]),
        pltpu.make_async_copy(cols_hbm, cols, in_sem.at[3]),
        pltpu.make_async_copy(count_hbm, count, in_sem.at[4]),
    ]
    loads[0].start()
    loads[1].start()
    peers = ([zh_peer(d) for d in range(1, NZH)] + [y_peer(d) for d in (4, 3, 5, 2, 6, 1, 7)] + [zl_peer(t) for t in order[:-1]]
             + [x_peer(d) for d in (2, 1, 3)] + [sibling])
    barrier = pltpu.get_barrier_semaphore()
    for peer in peers:
        pl.semaphore_signal(barrier, inc=1, device_id=peer, device_id_type=MESH)
    for load in loads[2:]:
        load.start()
    halves = [pltpu.make_async_copy(vals_hbm.at[0, 0, pl.ds(h * 32, 32)], vals.at[pl.ds(h * 32, 32)], val_sem.at[h])
              for h in range(2)]
    for load in halves:
        load.start()
    loads[0].wait()
    loads[1].wait()

    onehot = (lax.broadcasted_iota(jnp.int32, (TILE, TILE), 0) == reorder[...]).astype(F32)
    panel[0, 0, y] = lax.dot_general(feat[...], onehot, (((1,), (0,)), ((), ())), precision=lax.Precision.HIGHEST,
                                     preferred_element_type=F32)
    pl.semaphore_wait(barrier, len(peers))

    def remote(src, dst, send, recv, peer):
        return pltpu.make_async_remote_copy(src_ref=src, dst_ref=dst, send_sem=send, recv_sem=recv, device_id=peer,
                                            device_id_type=MESH)

    def await_bytes(ref, sem):
        pltpu.make_async_copy(ref, ref, sem).wait()

    def gather_own(h):
        mine = panel.at[h, 0, y]
        for e in range(1, NZH):
            remote(mine, panel.at[h, NZH - e, y], s_g.at[h], r_z.at[h], zh_peer(e)).start()
        for d in FAR + NEAR:
            recv = r_far.at[h, FAR.index(d)] if d in FAR else r_near.at[h]
            remote(mine, mine, s_g.at[h], recv, y_peer(d)).start()

    def gather_relay(h):
        await_bytes(panel.at[h, 0, pl.ds(0, NZH - 1)], r_z.at[h])
        for d, e in ((3, 2), (5, 1)):
            ref = panel.at[h, e, y]
            remote(ref, ref, s_g.at[h], r_relay.at[h], y_peer(d)).start()
        pair = panel.at[h, pl.ds(1, NZH - 1), y]
        for d in NEAR:
            remote(pair, pair, s_g.at[h], r_relay.at[h], y_peer(d)).start()
        for n, d, es in ((0, 4, (1, 2)), (1, 3, (2,)), (2, 5, (1,))):
            await_bytes(panel.at[h, 0, 0], r_far.at[h, n])
            k = (y + NY - d) & (NY - 1)
            for e in es:
                remote(panel.at[h, 0, k], panel.at[h, NZH - e, k], s_g.at[h], r_relay.at[h], zh_peer(e)).start()

    def split_panel(h, first, count):
        def one(k, carry):
            block = panel[h, k >> 3, k & (NY - 1)]
            high = block.astype(BF16)
            split[k, :, 0:TILE] = high
            split[k, :, TILE:2 * TILE] = (block - high.astype(F32)).astype(BF16)
            return carry
        lax.fori_loop(first, first + count, one, 0, unroll=8)

    def gather_end(h):
        await_bytes(panel.at[h, 0, pl.ds(0, len(NEAR))], r_near.at[h])
        split_panel(h, 0, NY)
        await_bytes(panel.at[h, pl.ds(1, NZH - 1), pl.ds(0, NY - 1)], r_relay.at[h])
        split_panel(h, NY, (NZH - 1) * NY)

    def prepare(first):
        def one(t, carry):
            tile = vals[t].T
            high = tile.astype(BF16)
            weights[t, :, 0:TILE] = high
            weights[t, :, TILE:2 * TILE] = (tile - high.astype(F32)).astype(BF16)
            return carry
        lax.fori_loop(first, first + 32, one, 0, unroll=4)

    def plan_slots():
        for load in loads[2:]:
            load.wait()
        lane = lax.broadcasted_iota(jnp.int32, (1, TILE), 1)
        pad = jnp.zeros((1, TILE - SLOTS), jnp.int32)
        group = jnp.where(lane < count[0, 0], jnp.concatenate([rows[0], pad], axis=1), 32)
        column = jnp.concatenate([cols[0], pad], axis=1)
        column_y = (column * 43) >> 7
        ahead = column - NZH * column_y - zh
        place = jnp.where(ahead < 0, ahead + NZH, ahead) * NY + column_y
        key = (group * TILE + lane) * 32 + place
        across = jnp.broadcast_to(key, (TILE, TILE))
        down = across.T
        rank = jnp.sum(jnp.where(across < down, 1, 0), axis=1, keepdims=True)
        lanes = lax.broadcasted_iota(jnp.int32, (TILE, TILE), 1)
        ordered = jnp.sum(jnp.where(rank == lanes, down, 0), axis=0, keepdims=True)
        upto = jnp.sum(jnp.where(down < (lanes + 1) * (TILE * 32), 1, 0), axis=0, keepdims=True)
        before = jnp.sum(jnp.where(down < lanes * (TILE * 32), 1, 0), axis=0, keepdims=True)
        table[0:1, :] = ordered
        table[1:2, :] = jnp.where(upto > before, upto - 1, SLOTS)

    def multiply():
        def one(k, carry):
            total, last = carry
            key = plan[0, k]
            group = key >> 12
            tile = weights[(key >> 5) & (SLOTS - 1)]
            left = split[jnp.minimum(key & 31, NY * NZH - 1)]
            high, low = tile[:, 0:TILE], tile[:, TILE:2 * TILE]
            term = lax.dot_general(left, jnp.concatenate([high, high], axis=0), (((1,), (0,)), ((), ())),
                                   preferred_element_type=F32)
            term = term + lax.dot_general(left[:, 0:TILE], low, (((1,), (0,)), ((), ())), preferred_element_type=F32)
            total = jnp.where(group == last, total, 0.0) + term
            seg[k] = total
            return total, group
        lax.fori_loop(0, SLOTS, one, (jnp.zeros((FEAT, TILE), F32), jnp.int32(-1)), unroll=32)

    def row_total(r):
        return seg[jnp.minimum(plan[1, r] & (TILE - 1), SLOTS)]

    def scatter_sum(h):
        for n, zt in enumerate(order):
            for xt in range(NX):
                send_a[h, n, xt] = row_total((xt * NZL + zt) * 2 + 1 - core)
            remote(send_a.at[h, n], got_a.at[h, n], s_a.at[h], r_a.at[h, n], sibling).start()
        for n, zt in enumerate(order):
            await_bytes(got_a.at[h, n], r_a.at[h, n])
            for d in (2, 1, 3):
                xt = (x + d) & (NX - 1)
                send_b[h, n, d - 1] = row_total((xt * NZL + zt) * 2 + core) + got_a[h, n, xt]
                remote(send_b.at[h, n, d - 1], got_b.at[h, n, d - 1], s_b.at[h], r_b.at[h, n], x_peer(d)).start()
            keep_b[n] = row_total((x * NZL + zt) * 2 + core) + got_a[h, n, x]
        for n, zt in enumerate(order):
            await_bytes(got_b.at[h, n], r_b.at[h, n])
            part = (keep_b[n] + got_b[h, n, 0]) + (got_b[h, n, 1] + got_b[h, n, 2])
            if n < NZL - 1:
                send_c[h, n] = part
                there = ((zl - zt + NZL) & (NZL - 1)) - 1
                remote(send_c.at[h, n], got_c.at[h, there], s_c.at[h], r_c.at[h], zl_peer(zt)).start()
        await_bytes(got_c.at[h], r_c.at[h])
        return part + (got_c[h, 0] + got_c[h, 1] + got_c[h, 2])

    def sends_end(h):
        await_bytes(panel.at[h, :, pl.ds(0, NY - 1)], s_g.at[h])
        await_bytes(panel.at[h, pl.ds(0, NZH - 1), 0], s_g.at[h])
        await_bytes(send_a.at[h], s_a.at[h])
        await_bytes(send_b.at[h], s_b.at[h])
        await_bytes(send_c.at[h], s_c.at[h])

    seg[SLOTS] = jnp.zeros((FEAT, TILE), F32)
    plan_copy = pltpu.make_async_copy(table, plan, plan_sem)

    def hop(h, carry):
        gather_own(h)

        @pl.when(h == 0)
        def _():
            plan_slots()
            plan_copy.start()
            halves[0].wait()
            prepare(0)

        gather_relay(h)

        @pl.when(h == 0)
        def _():
            halves[1].wait()
            prepare(32)
            plan_copy.wait()

        gather_end(h)
        multiply()
        field = scatter_sum(h)
        out_ref[h] = field

        @pl.when(h == 0)
        def _():
            panel[1, 0, y] = field

        return carry

    lax.fori_loop(0, 2, hop, 0)
    sends_end(0)
    sends_end(1)


def restore(fields_hbm, reorder_hbm, hop1_ref, hop2_ref, fields, reorder, sems):
    loads = [pltpu.make_async_copy(reorder_hbm, reorder, sems.at[0]), pltpu.make_async_copy(fields_hbm, fields, sems.at[1])]
    for load in loads:
        load.start()
    loads[0].wait()
    onehot = (lax.broadcasted_iota(jnp.int32, (TILE, TILE), 0) == reorder[...]).astype(F32)
    loads[1].wait()
    for n, hop in enumerate((hop1_ref, hop2_ref)):
        hop[...] = lax.dot_general(fields[n], onehot, (((1,), (1,)), ((), ())), precision=lax.Precision.HIGHEST,
                                   preferred_element_type=F32)


def shards(features, reorder, tile_rows, tile_cols, tile_vals, tile_count):
    dma = pltpu.SemaphoreType.DMA
    block = (FEAT, TILE)
    shape = jax.ShapeDtypeStruct(block, F32)
    fields = pl.pallas_call(
        kernel,
        name="two_hops",
        out_shape=jax.ShapeDtypeStruct((2,) + block, F32),
        in_specs=[pl.BlockSpec(memory_space=pltpu.HBM)] * 6,
        out_specs=pl.BlockSpec(memory_space=pltpu.VMEM),
        scratch_shapes=[
            pltpu.VMEM(block, F32),
            pltpu.VMEM((1, TILE), jnp.int32),
            pltpu.VMEM((1, 1, SLOTS), jnp.int32),
            pltpu.VMEM((1, 1, SLOTS), jnp.int32),
            pltpu.SMEM((1, 1), jnp.int32),
            pltpu.VMEM((SLOTS, TILE, TILE), F32),
            pltpu.VMEM((8, TILE), jnp.int32),
            pltpu.SMEM((8, TILE), jnp.int32),
            pltpu.VMEM((SLOTS, TILE, 2 * TILE), BF16),
            pltpu.VMEM((2, NZH, NY) + block, F32),
            pltpu.VMEM((NY * NZH, FEAT, 2 * TILE), BF16),
            pltpu.VMEM((SLOTS + 1,) + block, F32),
            pltpu.VMEM((2, NZL, NX) + block, F32),
            pltpu.VMEM((2, NZL, NX) + block, F32),
            pltpu.VMEM((2, NZL, NX - 1) + block, F32),
            pltpu.VMEM((2, NZL, NX - 1) + block, F32),
            pltpu.VMEM((NZL,) + block, F32),
            pltpu.VMEM((2, NZL - 1) + block, F32),
            pltpu.VMEM((2, NZL - 1) + block, F32),
            dma((5,)), dma((2,)), dma,
            dma((2,)), dma((2,)), dma((2, len(FAR))), dma((2,)), dma((2,)),
            dma((2,)), dma((2, NZL)), dma((2,)), dma((2, NZL)), dma((2,)), dma((2,)),
        ],
        compiler_params=pltpu.CompilerParams(collective_id=0, has_side_effects=True, vmem_limit_bytes=56 << 20),
        cost_estimate=pl.CostEstimate(flops=2 * 2 * 64 * 64 * 128 * 128 * 3, bytes_accessed=4 << 20, transcendentals=0),
    )(features, reorder, tile_rows, tile_cols, tile_count, tile_vals)
    return pl.pallas_call(
        restore,
        name="restore",
        out_shape=(shape, shape),
        in_specs=[pl.BlockSpec(memory_space=pltpu.HBM)] * 2,
        out_specs=(pl.BlockSpec(memory_space=pltpu.VMEM), pl.BlockSpec(memory_space=pltpu.VMEM)),
        scratch_shapes=[pltpu.VMEM((2,) + block, F32), pltpu.VMEM((1, TILE), jnp.int32), dma((2,))],
        compiler_params=pltpu.CompilerParams(vmem_limit_bytes=56 << 20),
    )(fields, reorder)


def solution(mesh):
    return jax.shard_map(
        shards,
        mesh=mesh,
        in_specs=(
            P(None, ("blk", "row")),
            P(("blk", "row"), None),
            P("blk", "row", None),
            P("blk", "row", None),
            P("blk", "row", None, None, None),
            P("blk", "row"),
        ),
        out_specs=(P(None, ("blk", "row")), P(None, ("blk", "row"))),
        check_vma=False,
    )
```

time: 83.8 us -> 75.2 us (0.90)
  Pallas kernels: 79.4 us -> 73.7 us
  local copies, waits for them, and re-layouts: 2.75 us -> 0 us
    pallas_call x1 -> x2, Pallas kernels: 79.4 us -> 73.7 us  [the longest x1 71.9 us: shards(): pl.pallas_call(kernel, name='two_hops', out_shape=jax.ShapeDtypeStruct((2...]
    unnamed x2 -> x0, local copies, waits for them, and re-layouts: 2.75 us -> none
where the time goes in v2:
time: 75.2 us; the launch traced here: 75 us
  Pallas kernels  73.7 us (98%)
  between operations  1.29 us (2%)
    pallas_call x1, Pallas kernels, shards(): pl.pallas_call(kernel, name='two_hops', out_shape=jax.ShapeDtypeStruct((2...  71.9 us
    pallas_call x1, Pallas kernels, shards(): pl.pallas_call(restore, name='restore', out_shape=(shape, shape), in_spec...  1.85 us

profile of v2, /device:TPU:1, one launch (start us, length us, event | category | flops | bytes accessed | tf_op | source)
XLA Modules:
  0.0 75.0 jit_solution(16183934771756291130)
XLA Ops:
  1.3 71.9 %two_hops.1.fields_hbm = f32[2,64,128]{2,1,0:T(8,128)} custom-call(f32[64,128]{1,0:T(8,128)} %feat_hbm.1, s32[1,128]{1,0:T(1,128)} %reorder_hbm.3, s32[1,1,64]{2,1,0:T(1,128)} %rows_hbm.1, s32[1,1,64]{2,1,0:T(1,128)} %cols_hbm.1, s32[1,1]{1,0:T(1,128)S(6)} %copy.8.count_hbm, f32[1,1,64,128,128]{4,3,2,1,0:T(8,128)} %vals_hbm.1), custom_call_target="tpu_custom_call" | custom-call | flops 805306368 | bytes 4194304 | tf_op jit(solution)/shard_map/two_hops/pallas_call | solution.py:252
  73.2 1.9 %restore.1 = (f32[64,128]{1,0:T(8,128)}, f32[64,128]{1,0:T(8,128)}) custom-call(f32[2,64,128]{2,1,0:T(8,128)} %two_hops.1.fields_hbm, s32[1,128]{1,0:T(1,128)} %reorder_hbm.3), custom_call_target="tpu_custom_call" | custom-call | tf_op jit(solution)/shard_map/restore/pallas_call | solution.py:285

commit v3 on v2

--- a/solution.py
+++ b/solution.py
@@ -14,6 +14,8 @@
 TILE = 128
 FAR = (4, 3, 5)
 NEAR = (2, 6, 1, 7)
+PARTS = 2
+GROUP = FEAT // PARTS
 
 
 def device(y, zh, x, zl, core):
@@ -23,7 +25,7 @@
 def kernel(feat_hbm, reorder_hbm, rows_hbm, cols_hbm, count_hbm, vals_hbm,
            out_ref,
            feat, reorder, rows, cols, count, vals, table, plan, weights,
-           panel, split, seg, send_a, got_a, send_b, got_b, keep_b, send_c, got_c,
+           panel, split, seg, send_a, got_a, send_b, got_b, send_c, got_c,
            in_sem, val_sem, plan_sem,
            s_g, r_z, r_far, r_near, r_relay, s_a, r_a, s_b, r_b, s_c, r_c):
     blk = lax.axis_index("blk")
@@ -82,26 +84,33 @@
         pltpu.make_async_copy(ref, ref, sem).wait()
 
     def gather_own(h):
+        for f in range(PARTS):
+            part = pl.ds(f * GROUP, GROUP)
+            mine = panel.at[h, 0, y, part]
+            for e in range(1, NZH):
+                remote(mine, panel.at[h, NZH - e, y, part], s_g.at[h], r_z.at[h, f], zh_peer(e)).start()
+            for n, d in enumerate(FAR):
+                remote(mine, mine, s_g.at[h], r_far.at[h, f, n], y_peer(d)).start()
         mine = panel.at[h, 0, y]
-        for e in range(1, NZH):
-            remote(mine, panel.at[h, NZH - e, y], s_g.at[h], r_z.at[h], zh_peer(e)).start()
-        for d in FAR + NEAR:
-            recv = r_far.at[h, FAR.index(d)] if d in FAR else r_near.at[h]
-            remote(mine, mine, s_g.at[h], recv, y_peer(d)).start()
+        for d in NEAR:
+            remote(mine, mine, s_g.at[h], r_near.at[h], y_peer(d)).start()
 
     def gather_relay(h):
-        await_bytes(panel.at[h, 0, pl.ds(0, NZH - 1)], r_z.at[h])
-        for d, e in ((3, 2), (5, 1)):
-            ref = panel.at[h, e, y]
-            remote(ref, ref, s_g.at[h], r_relay.at[h], y_peer(d)).start()
-        pair = panel.at[h, pl.ds(1, NZH - 1), y]
-        for d in NEAR:
-            remote(pair, pair, s_g.at[h], r_relay.at[h], y_peer(d)).start()
-        for n, d, es in ((0, 4, (1, 2)), (1, 3, (2,)), (2, 5, (1,))):
-            await_bytes(panel.at[h, 0, 0], r_far.at[h, n])
-            k = (y + NY - d) & (NY - 1)
-            for e in es:
-                remote(panel.at[h, 0, k], panel.at[h, NZH - e, k], s_g.at[h], r_relay.at[h], zh_peer(e)).start()
+        for f in range(PARTS):
+            part = pl.ds(f * GROUP, GROUP)
+            await_bytes(panel.at[h, 0, pl.ds(0, NZH - 1), part], r_z.at[h, f])
+            for d, e in ((3, 2), (5, 1)):
+                ref = panel.at[h, e, y, part]
+                remote(ref, ref, s_g.at[h], r_relay.at[h], y_peer(d)).start()
+            if f == PARTS - 1:
+                pair = panel.at[h, pl.ds(1, NZH - 1), y]
+                for d in NEAR:
+                    remote(pair, pair, s_g.at[h], r_relay.at[h], y_peer(d)).start()
+            for n, d, steps in ((0, 4, (1, 2)), (1, 3, (2,)), (2, 5, (1,))):
+                await_bytes(panel.at[h, 0, 0, part], r_far.at[h, f, n])
+                k = (y + NY - d) & (NY - 1)
+                for e in steps:
+                    remote(panel.at[h, 0, k, part], panel.at[h, NZH - e, k, part], s_g.at[h], r_relay.at[h], zh_peer(e)).start()
 
     def split_panel(h, first, count):
         def one(k, carry):
@@ -162,39 +171,44 @@
             total = jnp.where(group == last, total, 0.0) + term
             seg[k] = total
             return total, group
-        lax.fori_loop(0, SLOTS, one, (jnp.zeros((FEAT, TILE), F32), jnp.int32(-1)), unroll=32)
+        lax.fori_loop(0, SLOTS, one, (jnp.zeros((FEAT, TILE), F32), jnp.int32(-1)), unroll=64)
 
     def row_total(r):
         return seg[jnp.minimum(plan[1, r] & (TILE - 1), SLOTS)]
-
-    def scatter_sum(h):
-        for n, zt in enumerate(order):
-            for xt in range(NX):
-                send_a[h, n, xt] = row_total((xt * NZL + zt) * 2 + 1 - core)
-            remote(send_a.at[h, n], got_a.at[h, n], s_a.at[h], r_a.at[h, n], sibling).start()
-        for n, zt in enumerate(order):
-            await_bytes(got_a.at[h, n], r_a.at[h, n])
-            for d in (2, 1, 3):
-                xt = (x + d) & (NX - 1)
-                send_b[h, n, d - 1] = row_total((xt * NZL + zt) * 2 + core) + got_a[h, n, xt]
-                remote(send_b.at[h, n, d - 1], got_b.at[h, n, d - 1], s_b.at[h], r_b.at[h, n], x_peer(d)).start()
-            keep_b[n] = row_total((x * NZL + zt) * 2 + core) + got_a[h, n, x]
-        for n, zt in enumerate(order):
-            await_bytes(got_b.at[h, n], r_b.at[h, n])
-            part = (keep_b[n] + got_b[h, n, 0]) + (got_b[h, n, 1] + got_b[h, n, 2])
-            if n < NZL - 1:
-                send_c[h, n] = part
-                there = ((zl - zt + NZL) & (NZL - 1)) - 1
-                remote(send_c.at[h, n], got_c.at[h, there], s_c.at[h], r_c.at[h], zl_peer(zt)).start()
-        await_bytes(got_c.at[h], r_c.at[h])
-        return part + (got_c[h, 0] + got_c[h, 1] + got_c[h, 2])
 
     def sends_end(h):
         await_bytes(panel.at[h, :, pl.ds(0, NY - 1)], s_g.at[h])
         await_bytes(panel.at[h, pl.ds(0, NZH - 1), 0], s_g.at[h])
         await_bytes(send_a.at[h], s_a.at[h])
         await_bytes(send_b.at[h], s_b.at[h])
+
+    def scatter_sum(h):
+        for n, zt in enumerate(order):
+            for xt in range(NX):
+                send_a[h, n, xt] = row_total((xt * NZL + zt) * 2 + 1 - core)
+            if n == 0:
+                remote(send_a.at[h, 0], got_a.at[h, 0], s_a.at[h], r_a.at[h, 0], sibling).start()
+        rest = pl.ds(1, NZL - 1)
+        remote(send_a.at[h, rest], got_a.at[h, rest], s_a.at[h], r_a.at[h, 1], sibling).start()
+        for n, zt in enumerate(order):
+            if n < 2:
+                await_bytes(got_a.at[h, pl.ds(n, 1 if n == 0 else NZL - 1)], r_a.at[h, n])
+            for d in (2, 1, 3):
+                xt = (x + d) & (NX - 1)
+                send_b[h, n, d - 1] = row_total((xt * NZL + zt) * 2 + core) + got_a[h, n, xt]
+                remote(send_b.at[h, n, d - 1], got_b.at[h, n, d - 1], s_b.at[h], r_b.at[h, n], x_peer(d)).start()
+        for n, zt in enumerate(order):
+            kept = row_total((x * NZL + zt) * 2 + core) + got_a[h, n, x]
+            await_bytes(got_b.at[h, n], r_b.at[h, n])
+            part = (kept + got_b[h, n, 0]) + (got_b[h, n, 1] + got_b[h, n, 2])
+            if n < NZL - 1:
+                send_c[h, n] = part
+                there = ((zl - zt + NZL) & (NZL - 1)) - 1
+                remote(send_c.at[h, n], got_c.at[h, there], s_c.at[h], r_c.at[h], zl_peer(zt)).start()
+        sends_end(h)
+        await_bytes(got_c.at[h], r_c.at[h])
         await_bytes(send_c.at[h], s_c.at[h])
+        return part + (got_c[h, 0] + got_c[h, 1] + got_c[h, 2])
 
     seg[SLOTS] = jnp.zeros((FEAT, TILE), F32)
     plan_copy = pltpu.make_async_copy(table, plan, plan_sem)
@@ -229,8 +243,6 @@
         return carry
 
     lax.fori_loop(0, 2, hop, 0)
-    sends_end(0)
-    sends_end(1)
 
 
 def restore(fields_hbm, reorder_hbm, hop1_ref, hop2_ref, fields, reorder, sems):
@@ -272,11 +284,10 @@
             pltpu.VMEM((2, NZL, NX) + block, F32),
             pltpu.VMEM((2, NZL, NX - 1) + block, F32),
             pltpu.VMEM((2, NZL, NX - 1) + block, F32),
-            pltpu.VMEM((NZL,) + block, F32),
             pltpu.VMEM((2, NZL - 1) + block, F32),
             pltpu.VMEM((2, NZL - 1) + block, F32),
             dma((5,)), dma((2,)), dma,
-            dma((2,)), dma((2,)), dma((2, len(FAR))), dma((2,)), dma((2,)),
+            dma((2,)), dma((2, PARTS)), dma((2, PARTS, len(FAR))), dma((2,)), dma((2,)),
             dma((2,)), dma((2, NZL)), dma((2,)), dma((2, NZL)), dma((2,)), dma((2,)),
         ],
         compiler_params=pltpu.CompilerParams(collective_id=0, has_side_effects=True, vmem_limit_bytes=56 << 20),

time: 75.2 us -> 74.4 us (0.989)
  Pallas kernels: 73.7 us -> 72.9 us
    pallas_call x1, Pallas kernels: 71.9 us -> 71.1 us  [shards(): pl.pallas_call(kernel, name='two_hops', out_shape=jax.ShapeDtypeStruct((2...]
where the time goes in v3:
time: 74.4 us; the launch traced here: 74.2 us
  Pallas kernels  72.9 us (98%)
  between operations  1.29 us (2%)
    pallas_call x1, Pallas kernels, shards(): pl.pallas_call(kernel, name='two_hops', out_shape=jax.ShapeDtypeStruct((2...  71.1 us
    pallas_call x1, Pallas kernels, shards(): pl.pallas_call(restore, name='restore', out_shape=(shape, shape), in_spec...  1.85 us

profile of v3, /device:TPU:1, one launch (start us, length us, event | category | flops | bytes accessed | tf_op | source)
XLA Modules:
  0.0 74.2 jit_solution(9148749266896979811)
XLA Ops:
  1.3 71.1 %two_hops.1.fields_hbm = f32[2,64,128]{2,1,0:T(8,128)} custom-call(f32[64,128]{1,0:T(8,128)} %feat_hbm.1, s32[1,128]{1,0:T(1,128)} %reorder_hbm.3, s32[1,1,64]{2,1,0:T(1,128)} %rows_hbm.1, s32[1,1,64]{2,1,0:T(1,128)} %cols_hbm.1, s32[1,1]{1,0:T(1,128)S(6)} %copy.8.count_hbm, f32[1,1,64,128,128]{4,3,2,1,0:T(8,128)} %vals_hbm.1), custom_call_target="tpu_custom_call" | custom-call | flops 805306368 | bytes 4194304 | tf_op jit(solution)/shard_map/two_hops/pallas_call | solution.py:264
  72.4 1.9 %restore.1 = (f32[64,128]{1,0:T(8,128)}, f32[64,128]{1,0:T(8,128)}) custom-call(f32[2,64,128]{2,1,0:T(8,128)} %two_hops.1.fields_hbm, s32[1,128]{1,0:T(1,128)} %reorder_hbm.3), custom_call_target="tpu_custom_call" | custom-call | tf_op jit(solution)/shard_map/restore/pallas_call | solution.py:296
